TPU v7x, 32 devices: a whole 2x2x4 slice. The times are simulated.
32 devices in a mesh: blk: 8 (over y, x, core), grp: 4 (over z).
Axes of the slice: x: 2, y: 2, z: 4, core: 2. Of those that a mesh axis runs over, the one named last changes fastest.
Arguments:
- source_embed: bfloat16 [16384, 768], P(('blk', 'grp')), may hold values from -60 to 60
- target_embed: bfloat16 [1024, 768], P('blk'), may hold values from -18 to 18
- target_init: float32 [1024], P('blk'), may hold values from -6 to 6
- source_logw: float32 [16384], P(('blk', 'grp')), may hold values from -2 to 2
- target_logw: float32 [1024], P('blk'), may hold values from -2 to 2
Outputs:
- row_pot: float32 [16384], P(('blk', 'grp'))
- column_pot: float32 [1024], P('blk')
All inputs are finite; a program needn't handle non-finite values.
Results may differ from a plain program's by a relative error of at most 0.0003.
Values may be sent and summed in bfloat16 or wider, within the bound.
No kernel may reach another device: no remote copies, remote signals or barrier semaphores. Data moves between devices by JAX's collectives and lax.ppermute only.
A program may use at most 128 MiB of HBM per device.

v0:
```python
import math

import jax
import jax.numpy as jnp
from jax import lax
from jax.sharding import PartitionSpec as P

D = 768
ITERS = 2


epsilon = 0.1
inverse_eps = 10.0


def row_update(cost_matrix, column_pot, row_logw):
    scores = (column_pot[None, :] - cost_matrix) * inverse_eps
    row_top = jnp.max(scores, axis=1)
    row_sum = jnp.sum(jnp.exp(scores - row_top[:, None]), axis=1)
    return epsilon * row_logw - epsilon * (row_top + jnp.log(row_sum))


def shards(source_embed, target_embed, target_init, source_logw, target_logw):
    factor = -1.0 / math.sqrt(D)
    init_full, logw_full = (
        lax.all_gather(target_init, "blk", axis=0, tiled=True),
        lax.all_gather(target_logw, "blk", axis=0, tiled=True),
    )
    block_index = lax.axis_index("blk")
    rows_target = target_embed.shape[0]
    cost_matrix = (
        lax.dot_general(
            source_embed,
            lax.all_gather(target_embed, "blk", axis=0, tiled=True),
            (((1,), (1,)), ((), ())),
            preferred_element_type=jnp.float32,
        )
        * factor
    )
    column_pot = init_full
    row_pot = jnp.zeros(source_logw.shape, jnp.float32)
    for iteration in range(ITERS):
        row_pot = row_update(cost_matrix, column_pot, source_logw)
        scores = (row_pot[:, None] - cost_matrix) * inverse_eps
        col_top = jnp.max(scores, axis=0)
        col_peak = lax.pmax(col_top.astype(jnp.bfloat16), ("blk", "grp")).astype(col_top.dtype)
        col_total = lax.psum(jnp.sum(jnp.exp(scores - col_peak[None, :]), axis=0), ("blk", "grp"))
        column_pot = epsilon * logw_full - epsilon * (col_peak + jnp.log(col_total))
    return (
        row_pot,
        lax.dynamic_slice_in_dim(column_pot, block_index * rows_target, rows_target, 0),
    )


def solution(mesh):
    in_specs = (P(("blk", "grp"), None), P("blk", None), P("blk"), P(("blk", "grp")), P("blk"))
    out_specs = (P(("blk", "grp")), P("blk"))
    return jax.shard_map(shards, mesh=mesh, in_specs=in_specs, out_specs=out_specs, check_vma=False)
```

profile of v0, /device:TPU:0, one launch (start us, length us, event | category | flops | bytes accessed | tf_op | source)
XLA Modules:
  0.0 212.2 jit_solution(17412481426659578801)
XLA Ops:
  7.2 0.0 copy-start
  7.2 0.0 all-gather.4.cloned.1.call-start
  7.2 0.7 all-gather.4.cloned.1.call-update
  7.9 10.3 %all-gather.1 = f32[8,1,128]{2,1,0:T(1,128)S(1)} all-gather(f32[1,1,128]{2,1,0:T(1,128)} %bitcast.10), channel_id=1, replica_groups=mesh['blk'=8,'grp'=4] {'blk'}, dimensions={0}, use_global_device_ids=true | all-gather | bytes 4608 | tf_op jit(solution)/shard_map/all_gather | solution.py:26
  18.2 8.6 %all-gather = f32[8,1,128]{2,1,0:T(1,128)S(1)} all-gather(f32[1,1,128]{2,1,0:T(1,128)} %bitcast.11), channel_id=1, replica_groups=mesh['blk'=8,'grp'=4] {'blk'}, dimensions={0}, use_global_device_ids=true | all-gather | bytes 4608 | tf_op jit(solution)/shard_map/all_gather | solution.py:27
  26.8 11.5 %all-gather.4.cloned.1.call-done = bf16[1024,768]{1,0:T(8,128)(2,1)} async-done(((bf16[128,768]{1,0:T(8,128)(2,1)}), bf16[1024,768]{1,0:T(8,128)(2,1)}) %all-gather.4.cloned.1.call-update) | async-done | bytes 1572880 | tf_op jit(solution)/shard_map/all_gather | solution.py:34
  38.3 0.0 copy-done
  38.3 2.5 %fusion = (f32[512]{0:T(512)S(1)}, f32[512,1024]{1,0:T(8,128)S(1)}) fusion(f32[1024]{0:T(1024)S(1)} %bitcast.8, bf16[512,768]{1,0:T(8,128)(2,1)S(1)} %copy-done, bf16[1024,768]{1,0:T(8,128)(2,1)} %all-gather.4.cloned.1.call-done), kind=kOutput, calls=%fused_computation.8 | convolution fusion | flops 807403008 | bytes 4462592 | tf_op jit(solution)/shard_map/dot_general | solution.py:32
  40.8 0.0 copy-start.2
  40.9 0.6 exponential_reduce_fusion.3
  41.4 0.1 copy-done.2
  41.5 0.3 fusion.1
  41.8 39.4 %pmax.14 = bf16[1024]{0:T(1024)(128)(2,1)S(1)} all-reduce(bf16[1024]{0:T(1024)(128)(2,1)S(1)} %fusion.1), channel_id=1, replica_groups=mesh['blk'=8,'grp'=4] {'blk','grp'}, use_global_device_ids=true, to_apply=%region_3.0 | all-reduce | flops 1024 | bytes 4096 | tf_op jit(solution)/shard_map/pmax | solution.py:46
  81.3 0.5 exponential_reduce_fusion.2
  81.8 41.0 %psum.14 = f32[1024]{0:T(1024)S(1)} all-reduce(f32[1024]{0:T(1024)S(1)} %exponential_reduce_fusion.2), channel_id=1, replica_groups=mesh['blk'=8,'grp'=4] {'blk','grp'}, use_global_device_ids=true, to_apply=%region_5.0 | all-reduce | flops 1024 | bytes 8192 | tf_op jit(solution)/shard_map/psum | solution.py:47
  122.8 0.3 fusion.2
  123.1 0.6 exponential_reduce_fusion.1
  123.7 0.0 copy-start.1
  123.7 0.3 fusion.3
  124.0 39.2 %pmax.15 = bf16[1024]{0:T(1024)(128)(2,1)S(1)} all-reduce(bf16[1024]{0:T(1024)(128)(2,1)S(1)} %fusion.3), channel_id=1, replica_groups=mesh['blk'=8,'grp'=4] {'blk','grp'}, use_global_device_ids=true, to_apply=%region_9.0 | all-reduce | flops 1024 | bytes 4096 | tf_op jit(solution)/shard_map/pmax | solution.py:46
  163.2 0.5 exponential_reduce_fusion
  163.7 0.0 copy-done.1
  163.7 41.0 %psum.15 = f32[1024]{0:T(1024)S(1)} all-reduce(f32[1024]{0:T(1024)S(1)} %exponential_reduce_fusion), channel_id=1, replica_groups=mesh['blk'=8,'grp'=4] {'blk','grp'}, use_global_device_ids=true, to_apply=%region_11.0 | all-reduce | flops 1024 | bytes 8192 | tf_op jit(solution)/shard_map/psum | solution.py:47
  204.7 0.6 dynamic_slice.3
  (7 shorter events, 0.0 us)
Async XLA Ops:
  7.2 31.2 %copy-start = (bf16[512,768]{1,0:T(8,128)(2,1)S(1)}, bf16[512,768]{1,0:T(8,128)(2,1)}, u32[]{:S(2)}) copy-start(bf16[512,768]{1,0:T(8,128)(2,1)} %param.5) | copy-start | bytes 2359300
  7.2 31.1 %all-gather.4.cloned.1.call-start = ((), (), s32[]{:S(2)}) async-start(), calls=%async_computation | async-start | bytes 1769472 | tf_op jit(solution)/shard_map/all_gather | solution.py:34
  40.8 0.7 copy-start.2
  123.7 40.0 %copy-start.1 = (f32[512]{0:T(512)}, f32[512]{0:T(512)S(1)}, u32[]{:S(2)}) copy-start(f32[512]{0:T(512)S(1)} %multiply_subtract_fusion.2) | copy-start | bytes 6148
Sparse Core Ops, SparseCore 0:
  9.9 28.3 all-gather.3
where the time goes:
time: 213 us; the launch traced here: 212 us
  blocking collectives  180 us (85%)
  between operations  14.1 us (7%)
  waiting for transfers between devices  12.2 us (6%)
  other arithmetic  3.05 us (1%)
  matrix products  2.51 us (1%)
    psum x2, blocking collectives, shards(): lax.psum(jnp.sum(jnp.exp(scores - col_peak[None, :]), axis=0), ('blk', 'g...  82.1 us
    pmax x2, blocking collectives, shards(): lax.pmax(col_top.astype(jnp.bfloat16), ('blk', 'grp')).astype(col_top.dtype)  78.6 us
    all_gather x1, waiting for transfers between devices, shards(): lax.all_gather(target_embed, 'blk', axis=0, tiled=True)  11.5 us
    all_gather x1, blocking collectives, shards(): lax.all_gather(target_init, 'blk', axis=0, tiled=True)  10.3 us
    all_gather x1, blocking collectives, shards(): lax.all_gather(target_logw, 'blk', axis=0, tiled=True)  8.61 us
  transfers between devices with their start and end apart: 1, of which 1 were waited for; matrix products, arithmetic and copies ran while one was open for 0% of the time, Pallas kernels for 0%

commit v1 on v0

v1 whole, which is shorter than its diff:
```python
import math

import jax
import jax.numpy as jnp
from jax import lax
from jax.sharding import PartitionSpec as P

ITERS = 2
epsilon = 0.1
inverse_eps = 10.0


def partner(index, step, size):
    return index ^ step if size & (size - 1) == 0 else (index + step) % size


def moved(position, step, size):
    return position ^ step if size & (size - 1) == 0 else (position - step) % size


def fetch(array, axis, step, size):
    return lax.ppermute(array, axis, [(partner(i, step, size), i) for i in range(size)])


def gather_positions(array, axis, size):
    if size % 2 or size & (size - 1):
        return [array] + [fetch(array, axis, step, size) for step in range(1, size)]
    even = {0: array}
    for step in range(2, size, 2):
        even[step] = fetch(array, axis, step, size)
    odd = {step + 1: fetch(block, axis, 1, size) for step, block in even.items()}
    return [block for _, block in sorted({**even, **odd}.items())]


def lse(values):
    top = jnp.max(values, axis=0)
    return top + jnp.log(jnp.sum(jnp.exp(values - top[None, :]), axis=0))


def solution(mesh):
    blk, grp = mesh.shape["blk"], mesh.shape["grp"]

    def shards(source_embed, target_embed, target_init, source_logw, target_logw):
        width = target_embed.shape[0]
        factor = -1.0 / math.sqrt(source_embed.shape[1])
        small = jnp.stack([target_init, target_logw])
        smalls = [small] + [fetch(small, "blk", step, blk) for step in range(1, blk)]
        smalls = jnp.concatenate(smalls, axis=1)
        init_all, logw_all = smalls[0], smalls[1]
        targets = jnp.concatenate(gather_positions(target_embed, "blk", blk), axis=0)
        cost = (
            lax.dot_general(
                source_embed, targets, (((1,), (1,)), ((), ())), preferred_element_type=jnp.float32
            )
            * factor
        )

        def column_lse(row_pot):
            scores = (row_pot[:, None] - cost) * inverse_eps
            return lse(scores)

        def over_grp(part):
            return lse(jnp.stack([part] + [fetch(part, "grp", s, grp) for s in range(1, grp)]))

        column_pot = init_all
        for iteration in range(ITERS):
            scores = (column_pot[None, :] - cost) * inverse_eps
            row_top = jnp.max(scores, axis=1)
            row_sum = jnp.sum(jnp.exp(scores - row_top[:, None]), axis=1)
            row_pot = epsilon * source_logw - epsilon * (row_top + jnp.log(row_sum))
            part = column_lse(row_pot)
            if iteration < ITERS - 1:
                blocks = part.reshape(blk, width)
                parts = [part]
                for step in range(1, blk):
                    got = fetch(part, "blk", step, blk).reshape(blk, width)
                    parts.append(
                        jnp.concatenate([got[moved(p, step, blk)] for p in range(blk)])
                    )
                total = over_grp(lse(jnp.stack(parts)))
                column_pot = epsilon * logw_all - epsilon * total
            else:
                blocks = part.reshape(blk, width)
                parts = [blocks[0]]
                for step in range(1, blk):
                    parts.append(fetch(blocks[moved(0, step, blk)], "blk", step, blk))
                total = over_grp(lse(jnp.stack(parts)))
                own_column = epsilon * target_logw - epsilon * total
        return row_pot, own_column

    in_specs = (P(("blk", "grp"), None), P("blk", None), P("blk"), P(("blk", "grp")), P("blk"))
    out_specs = (P(("blk", "grp")), P("blk"))
    return jax.shard_map(shards, mesh=mesh, in_specs=in_specs, out_specs=out_specs, check_vma=False)
```

time: 213 us -> 64.8 us (0.30)
  blocking collectives: 180 us -> 0 us
  starting transfers between devices: 0.04 us -> 34.5 us
  between operations: 14.1 us -> 1.26 us
  waiting for transfers between devices: 12.2 us -> 21.3 us
    psum x2 -> x0, blocking collectives: 82.1 us -> none  [shards(): lax.psum(jnp.sum(jnp.exp(scores - col_peak[None, :]), axis=0), ('blk', 'g...]
    pmax x2 -> x0, blocking collectives: 78.6 us -> none  [shards(): lax.pmax(col_top.astype(jnp.bfloat16), ('blk', 'grp')).astype(col_top.dtype)]
    ppermute x0 -> x34, starting transfers between devices: none -> 34.5 us  [fetch(): lax.ppermute(array, axis, [(partner(i, step, size), i) for i in range(siz...]
    ppermute x0 -> x34, waiting for transfers between devices: none -> 21.3 us  [fetch(): lax.ppermute(array, axis, [(partner(i, step, size), i) for i in range(siz...]
    all_gather x2 -> x0, blocking collectives: 18.9 us -> none  [the longest x1 10.3 us: shards(): lax.all_gather(target_init, 'blk', axis=0, tiled=True)]
    all_gather x1 -> x0, waiting for transfers between devices: 11.5 us -> none  [shards(): lax.all_gather(target_embed, 'blk', axis=0, tiled=True)]
  transfers between devices with their start and end apart: 1 -> 34, of which waited for: 1 -> 12; matrix products, arithmetic and copies ran while one was open for 0% -> 3% of each run, Pallas kernels for 0% -> 0%
where the time goes in v1:
time: 64.8 us; the launch traced here: 64.6 us
  starting transfers between devices  34.5 us (53%)
  waiting for transfers between devices  21.3 us (33%)
  other arithmetic  4.58 us (7%)
  local copies, waits for them, and re-layouts  1.93 us (3%)
  between operations  1.26 us (2%)
  matrix products  1.03 us (2%)
    ppermute x34, starting transfers between devices, fetch(): lax.ppermute(array, axis, [(partner(i, step, size), i) for i in range(siz...  34.5 us
    ppermute x34, waiting for transfers between devices, fetch(): lax.ppermute(array, axis, [(partner(i, step, size), i) for i in range(siz...  21.3 us
    unnamed x77, local copies, waits for them, and re-layouts  1.73 us
    reduce_sum x6, other arithmetic, lse(): return top + jnp.log(jnp.sum(jnp.exp(values - top[None, :]), axis=0))  1.31 us
  transfers between devices with their start and end apart: 34, of which 12 were waited for; matrix products, arithmetic and copies ran while one was open for 3% of the time, Pallas kernels for 0%

profile of v1, /device:TPU:0, one launch (start us, length us, event | category | flops | bytes accessed | tf_op | source)
XLA Modules:
  0.0 64.6 jit_solution(156638689422938037)
XLA Ops:
  0.6 0.8 %pad_maximum_fusion.3 = (f32[2,128]{1,0:T(2,128)S(1)}, f32[2,1024]{1,0:T(2,128)S(1)}) fusion(f32[1,128]{1,0:T(1,128)} %bitcast.145, f32[1,128]{1,0:T(1,128)} %bitcast.146), kind=kLoop, calls=%fused_computation.119 | loop fusion | flops 255 | bytes 3072 | tf_op jit(solution)/shard_map/stack | solution.py:46
  1.4 0.5 collective-permute-start
  1.9 2.6 %collective-permute-start.1 = (f32[2,128]{1,0:T(2,128)S(1)}, f32[2,128]{1,0:T(2,128)S(1)}, u32[]{:S(2)}, u32[]{:S(2)}) collective-permute-start(f32[2,128]{1,0:T(2,128)S(1)} %get-tuple-element.24), channel_id=1, source_target_pairs={{8,0},{12,4},{0,8},{4,12},{24,16},{28,20},{16,24},{20,28},{9,1},{1... | collective-permute-start | bytes 3080 | tf_op jit(solution)/shard_map/ppermute | solution.py:22
  4.5 1.8 %collective-permute-start.3 = (f32[2,128]{1,0:T(2,128)S(1)}, f32[2,128]{1,0:T(2,128)S(1)}, u32[]{:S(2)}, u32[]{:S(2)}) collective-permute-start(f32[2,128]{1,0:T(2,128)S(1)} %get-tuple-element.24), channel_id=1, source_target_pairs={{16,0},{20,4},{24,8},{28,12},{0,16},{4,20},{8,24},{12,28},{17,1},{... | collective-permute-start | bytes 3080 | tf_op jit(solution)/shard_map/ppermute | solution.py:22
  6.2 0.9 %constant_dynamic-update-slice_fusion.15 = bf16[1024,768]{1,0:T(8,128)(2,1)S(1)} fusion(bf16[128,768]{1,0:T(8,128)(2,1)} %param.6), kind=kLoop, calls=%fused_computation.28 | loop fusion | bytes 393216
  7.2 2.7 %collective-permute-start.5 = (f32[2,128]{1,0:T(2,128)S(1)}, f32[2,128]{1,0:T(2,128)S(1)}, u32[]{:S(2)}, u32[]{:S(2)}) collective-permute-start(f32[2,128]{1,0:T(2,128)S(1)} %get-tuple-element.24), channel_id=1, source_target_pairs={{24,0},{28,4},{16,8},{20,12},{8,16},{12,20},{0,24},{4,28},{25,1},{... | collective-permute-start | bytes 3080 | tf_op jit(solution)/shard_map/ppermute | solution.py:22
  9.9 0.1 collective-permute-start.6
  10.0 1.6 %collective-permute-start.8 = (bf16[128,768]{1,0:T(8,128)(2,1)}, bf16[128,768]{1,0:T(8,128)(2,1)S(1)}, u32[]{:S(2)}, u32[]{:S(2)}) collective-permute-start(bf16[128,768]{1,0:T(8,128)(2,1)} %param.6), channel_id=1, source_target_pairs={{8,0},{12,4},{0,8},{4,12},{24,16},{28,20},{16,24},{20,28},{9,1},{1... | collective-permute-start | bytes 589832 | tf_op jit(solution)/shard_map/ppermute | solution.py:22
  11.7 1.5 %collective-permute-start.10 = (bf16[128,768]{1,0:T(8,128)(2,1)}, bf16[128,768]{1,0:T(8,128)(2,1)S(1)}, u32[]{:S(2)}, u32[]{:S(2)}) collective-permute-start(bf16[128,768]{1,0:T(8,128)(2,1)} %param.6), channel_id=1, source_target_pairs={{16,0},{20,4},{24,8},{28,12},{0,16},{4,20},{8,24},{12,28},{17,1},{... | collective-permute-start | bytes 589832 | tf_op jit(solution)/shard_map/ppermute | solution.py:22
  13.3 1.1 %collective-permute-start.12 = (bf16[128,768]{1,0:T(8,128)(2,1)}, bf16[128,768]{1,0:T(8,128)(2,1)S(1)}, u32[]{:S(2)}, u32[]{:S(2)}) collective-permute-start(bf16[128,768]{1,0:T(8,128)(2,1)} %param.6), channel_id=1, source_target_pairs={{24,0},{28,4},{16,8},{20,12},{8,16},{12,20},{0,24},{4,28},{25,1},{... | collective-permute-start | bytes 589832 | tf_op jit(solution)/shard_map/ppermute | solution.py:22
  14.4 3.6 %collective-permute-done.8 = bf16[128,768]{1,0:T(8,128)(2,1)S(1)} collective-permute-done((bf16[128,768]{1,0:T(8,128)(2,1)}, bf16[128,768]{1,0:T(8,128)(2,1)S(1)}, u32[]{:S(2)}, u32[]{:S(2)}) %collective-permute-start.8) | collective-permute-done | bytes 196640 | tf_op jit(solution)/shard_map/ppermute | solution.py:22
  18.0 5.4 %collective-permute-done.10 = bf16[128,768]{1,0:T(8,128)(2,1)S(1)} collective-permute-done((bf16[128,768]{1,0:T(8,128)(2,1)}, bf16[128,768]{1,0:T(8,128)(2,1)S(1)}, u32[]{:S(2)}, u32[]{:S(2)}) %collective-permute-start.10) | collective-permute-done | bytes 196640 | tf_op jit(solution)/shard_map/ppermute | solution.py:22
  23.4 0.5 collective-permute-start.13
  24.0 0.8 %collective-permute-done.11 = bf16[128,768]{1,0:T(8,128)(2,1)S(1)} collective-permute-done((bf16[128,768]{1,0:T(8,128)(2,1)S(1)}, bf16[128,768]{1,0:T(8,128)(2,1)S(1)}, u32[]{:S(2)}, u32[]{:S(2)}) %collective-permute-start.11) | collective-permute-done | bytes 196640 | tf_op jit(solution)/shard_map/ppermute | solution.py:22
  24.9 0.2 collective-permute-done.13
  25.2 1.0 %fusion = (f32[512]{0:T(512)S(1)}, f32[1024,512]{1,0:T(8,128)S(1)}) fusion(f32[1024]{0:T(1024)S(1)} %bitcast.112, bf16[1024,768]{1,0:T(8,128)(2,1)S(1)} %constant_dynamic-update-slice_fusion.8, bf16[512,768]{1,0:T(8,128)(2,1)S(1)} %copy-done), kind=kOutput, calls=%fused_computation.8 | convolution fusion | flops 807403008 | bytes 4462592 | tf_op jit(solution)/shard_map/dot_general | solution.py:52
  26.2 0.5 exponential_reduce_fusion.3
  26.7 0.2 copy-done.2
  26.9 0.3 fusion.1
  27.2 0.6 exponential_reduce_fusion.2
  27.8 1.4 %collective-permute-start.20 = (f32[1024]{0:T(1024)S(1)}, f32[1024]{0:T(1024)S(1)}, u32[]{:S(2)}, u32[]{:S(2)}) collective-permute-start(f32[1024]{0:T(1024)S(1)} %log_add_fusion.1), channel_id=1, source_target_pairs={{28,0},{24,4},{20,8},{16,12},{12,16},{8,20},{4,24},{0,28},{29,1},{... | collective-permute-start | bytes 12296 | tf_op jit(solution)/shard_map/ppermute | solution.py:22
  29.2 0.3 collective-permute-start.14
  29.5 1.3 %collective-permute-start.16 = (f32[1024]{0:T(1024)S(1)}, f32[1024]{0:T(1024)S(1)}, u32[]{:S(2)}, u32[]{:S(2)}) collective-permute-start(f32[1024]{0:T(1024)S(1)} %log_add_fusion.1), channel_id=1, source_target_pairs={{12,0},{8,4},{4,8},{0,12},{28,16},{24,20},{20,24},{16,28},{13,1},{... | collective-permute-start | bytes 12296 | tf_op jit(solution)/shard_map/ppermute | solution.py:22
  30.8 0.4 collective-permute-start.18
  31.2 0.5 collective-permute-start.15
  31.8 2.4 %collective-permute-start.19 = (f32[1024]{0:T(1024)S(1)}, f32[1024]{0:T(1024)S(1)}, u32[]{:S(2)}, u32[]{:S(2)}) collective-permute-start(f32[1024]{0:T(1024)S(1)} %log_add_fusion.1), channel_id=1, source_target_pairs={{24,0},{28,4},{16,8},{20,12},{8,16},{12,20},{0,24},{4,28},{25,1},{... | collective-permute-start | bytes 12296 | tf_op jit(solution)/shard_map/ppermute | solution.py:22
  34.3 0.6 collective-permute-start.17
  35.2 2.8 %collective-permute-done.17 = f32[1024]{0:T(1024)S(1)} collective-permute-done((f32[1024]{0:T(1024)S(1)}, f32[1024]{0:T(1024)S(1)}, u32[]{:S(2)}, u32[]{:S(2)}) %collective-permute-start.17) | collective-permute-done | bytes 4128 | tf_op jit(solution)/shard_map/ppermute | solution.py:22
  38.2 1.6 %collective-permute-start.21 = (f32[1024]{0:T(1024)S(1)}, f32[1024]{0:T(1024)S(1)}, u32[]{:S(2)}, u32[]{:S(2)}) collective-permute-start(f32[1024]{0:T(1024)S(1)} %get-tuple-element.11), channel_id=1, source_target_pairs={{1,0},{0,1},{3,2},{2,3},{5,4},{4,5},{7,6},{6,7},{9,8},{8,9},{11,10... | collective-permute-start | bytes 12296 | tf_op jit(solution)/shard_map/ppermute | solution.py:22
  39.8 2.6 %collective-permute-start.22 = (f32[1024]{0:T(1024)S(1)}, f32[1024]{0:T(1024)S(1)}, u32[]{:S(2)}, u32[]{:S(2)}) collective-permute-start(f32[1024]{0:T(1024)S(1)} %get-tuple-element.11), channel_id=1, source_target_pairs={{2,0},{3,1},{0,2},{1,3},{6,4},{7,5},{4,6},{5,7},{10,8},{11,9},{8,1... | collective-permute-start | bytes 12296 | tf_op jit(solution)/shard_map/ppermute | solution.py:22
  42.4 0.2 collective-permute-start.23
  43.1 1.3 %collective-permute-done.22 = f32[1024]{0:T(1024)S(1)} collective-permute-done((f32[1024]{0:T(1024)S(1)}, f32[1024]{0:T(1024)S(1)}, u32[]{:S(2)}, u32[]{:S(2)}) %collective-permute-start.22) | collective-permute-done | bytes 4128 | tf_op jit(solution)/shard_map/ppermute | solution.py:22
  44.3 3.5 %collective-permute-done.23 = f32[1024]{0:T(1024)S(1)} collective-permute-done((f32[1024]{0:T(1024)S(1)}, f32[1024]{0:T(1024)S(1)}, u32[]{:S(2)}, u32[]{:S(2)}) %collective-permute-start.23) | collective-permute-done | bytes 4128 | tf_op jit(solution)/shard_map/ppermute | solution.py:22
  47.9 0.3 fusion.2
  48.2 0.5 exponential_reduce_fusion.1
  48.7 0.3 fusion.3
  49.0 0.6 exponential_reduce_fusion
  49.7 0.7 %collective-permute-start.25 = (f32[128]{0:T(128)S(1)}, f32[128]{0:T(128)S(1)}, u32[]{:S(2)}, u32[]{:S(2)}) collective-permute-start(f32[128]{0:T(128)S(1)} %get-tuple-element.8), channel_id=1, source_target_pairs={{8,0},{12,4},{0,8},{4,12},{24,16},{28,20},{16,24},{20,28},{9,1},{1... | collective-permute-start | bytes 1544 | tf_op jit(solution)/shard_map/ppermute | solution.py:22
  50.4 1.2 %collective-permute-start.26 = (f32[128]{0:T(128)S(1)}, f32[128]{0:T(128)S(1)}, u32[]{:S(2)}, u32[]{:S(2)}) collective-permute-start(f32[128]{0:T(128)S(1)} %get-tuple-element.7), channel_id=1, source_target_pairs={{12,0},{8,4},{4,8},{0,12},{28,16},{24,20},{20,24},{16,28},{13,1},{... | collective-permute-start | bytes 1544 | tf_op jit(solution)/shard_map/ppermute | solution.py:22
  51.6 0.5 collective-permute-start.27
  52.1 1.2 %collective-permute-start.28 = (f32[128]{0:T(128)S(1)}, f32[128]{0:T(128)S(1)}, u32[]{:S(2)}, u32[]{:S(2)}) collective-permute-start(f32[128]{0:T(128)S(1)} %get-tuple-element.5), channel_id=1, source_target_pairs={{20,0},{16,4},{28,8},{24,12},{4,16},{0,20},{12,24},{8,28},{21,1},{... | collective-permute-start | bytes 1544 | tf_op jit(solution)/shard_map/ppermute | solution.py:22
  53.3 0.6 %collective-permute-start.29 = (f32[128]{0:T(128)S(1)}, f32[128]{0:T(128)S(1)}, u32[]{:S(2)}, u32[]{:S(2)}) collective-permute-start(f32[128]{0:T(128)S(1)} %get-tuple-element.4), channel_id=1, source_target_pairs={{24,0},{28,4},{16,8},{20,12},{8,16},{12,20},{0,24},{4,28},{25,1},{... | collective-permute-start | bytes 1544 | tf_op jit(solution)/shard_map/ppermute | solution.py:22
  53.9 2.0 %collective-permute-start.30 = (f32[128]{0:T(128)S(1)}, f32[128]{0:T(128)S(1)}, u32[]{:S(2)}, u32[]{:S(2)}) collective-permute-start(f32[128]{0:T(128)S(1)} %get-tuple-element.3), channel_id=1, source_target_pairs={{28,0},{24,4},{20,8},{16,12},{12,16},{8,20},{4,24},{0,28},{29,1},{... | collective-permute-start | bytes 1544 | tf_op jit(solution)/shard_map/ppermute | solution.py:22
  56.0 1.7 %collective-permute-done.29 = f32[128]{0:T(128)S(1)} collective-permute-done((f32[128]{0:T(128)S(1)}, f32[128]{0:T(128)S(1)}, u32[]{:S(2)}, u32[]{:S(2)}) %collective-permute-start.29) | collective-permute-done | bytes 544 | tf_op jit(solution)/shard_map/ppermute | solution.py:22
  57.9 0.8 %collective-permute-start.32 = (f32[128]{0:T(128)S(1)}, f32[128]{0:T(128)S(1)}, u32[]{:S(2)}, u32[]{:S(2)}) collective-permute-start(f32[128]{0:T(128)S(1)} %log_add_fusion.2), channel_id=1, source_target_pairs={{2,0},{3,1},{0,2},{1,3},{6,4},{7,5},{4,6},{5,7},{10,8},{11,9},{8,1... | collective-permute-start | bytes 1544 | tf_op jit(solution)/shard_map/ppermute | solution.py:22
  58.7 3.6 %collective-permute-start.33 = (f32[128]{0:T(128)S(1)}, f32[128]{0:T(128)S(1)}, u32[]{:S(2)}, u32[]{:S(2)}) collective-permute-start(f32[128]{0:T(128)S(1)} %log_add_fusion.2), channel_id=1, source_target_pairs={{3,0},{2,1},{1,2},{0,3},{7,4},{6,5},{5,6},{4,7},{11,8},{10,9},{9,1... | collective-permute-start | bytes 1544 | tf_op jit(solution)/shard_map/ppermute | solution.py:22
  62.4 1.6 %collective-permute-done.33 = f32[128]{0:T(128)S(1)} collective-permute-done((f32[128]{0:T(128)S(1)}, f32[128]{0:T(128)S(1)}, u32[]{:S(2)}, u32[]{:S(2)}) %collective-permute-start.33) | collective-permute-done | bytes 544 | tf_op jit(solution)/shard_map/ppermute | solution.py:22
  64.1 0.5 multiply_subtract_fusion.2
  (147 shorter events, 1.8 us)
Async XLA Ops:
  0.6 24.5 %copy-start = (bf16[512,768]{1,0:T(8,128)(2,1)S(1)}, bf16[512,768]{1,0:T(8,128)(2,1)}, u32[]{:S(2)}) copy-start(bf16[512,768]{1,0:T(8,128)(2,1)} %param.5) | copy-start | bytes 2359300
  1.4 5.8 %collective-permute-start = (f32[2,128]{1,0:T(2,128)S(1)}, f32[2,128]{1,0:T(2,128)S(1)}, u32[]{:S(2)}, u32[]{:S(2)}) collective-permute-start(f32[2,128]{1,0:T(2,128)S(1)} %get-tuple-element.24), channel_id=1, source_target_pairs={{4,0},{0,4},{12,8},{8,12},{20,16},{16,20},{28,24},{24,28},{5,1},{1... | collective-permute-start | bytes 3080 | tf_op jit(solution)/shard_map/ppermute | solution.py:22
  1.9 8.0 %collective-permute-start.1 = (f32[2,128]{1,0:T(2,128)S(1)}, f32[2,128]{1,0:T(2,128)S(1)}, u32[]{:S(2)}, u32[]{:S(2)}) collective-permute-start(f32[2,128]{1,0:T(2,128)S(1)} %get-tuple-element.24), channel_id=1, source_target_pairs={{8,0},{12,4},{0,8},{4,12},{24,16},{28,20},{16,24},{20,28},{9,1},{1... | collective-permute-start | bytes 3080 | tf_op jit(solution)/shard_map/ppermute | solution.py:22
  4.4 5.6 %collective-permute-start.2 = (f32[2,128]{1,0:T(2,128)S(1)}, f32[2,128]{1,0:T(2,128)S(1)}, u32[]{:S(2)}, u32[]{:S(2)}) collective-permute-start(f32[2,128]{1,0:T(2,128)S(1)} %get-tuple-element.24), channel_id=1, source_target_pairs={{12,0},{8,4},{4,8},{0,12},{28,16},{24,20},{20,24},{16,28},{13,1},{... | collective-permute-start | bytes 3080 | tf_op jit(solution)/shard_map/ppermute | solution.py:22
  4.5 7.2 %collective-permute-start.3 = (f32[2,128]{1,0:T(2,128)S(1)}, f32[2,128]{1,0:T(2,128)S(1)}, u32[]{:S(2)}, u32[]{:S(2)}) collective-permute-start(f32[2,128]{1,0:T(2,128)S(1)} %get-tuple-element.24), channel_id=1, source_target_pairs={{16,0},{20,4},{24,8},{28,12},{0,16},{4,20},{8,24},{12,28},{17,1},{... | collective-permute-start | bytes 3080 | tf_op jit(solution)/shard_map/ppermute | solution.py:22
  6.2 5.5 %collective-permute-start.4 = (f32[2,128]{1,0:T(2,128)S(1)}, f32[2,128]{1,0:T(2,128)S(1)}, u32[]{:S(2)}, u32[]{:S(2)}) collective-permute-start(f32[2,128]{1,0:T(2,128)S(1)} %get-tuple-element.24), channel_id=1, source_target_pairs={{20,0},{16,4},{28,8},{24,12},{4,16},{0,20},{12,24},{8,28},{21,1},{... | collective-permute-start | bytes 3080 | tf_op jit(solution)/shard_map/ppermute | solution.py:22
  7.2 6.1 %collective-permute-start.5 = (f32[2,128]{1,0:T(2,128)S(1)}, f32[2,128]{1,0:T(2,128)S(1)}, u32[]{:S(2)}, u32[]{:S(2)}) collective-permute-start(f32[2,128]{1,0:T(2,128)S(1)} %get-tuple-element.24), channel_id=1, source_target_pairs={{24,0},{28,4},{16,8},{20,12},{8,16},{12,20},{0,24},{4,28},{25,1},{... | collective-permute-start | bytes 3080 | tf_op jit(solution)/shard_map/ppermute | solution.py:22
  9.9 4.5 %collective-permute-start.6 = (f32[2,128]{1,0:T(2,128)S(1)}, f32[2,128]{1,0:T(2,128)S(1)}, u32[]{:S(2)}, u32[]{:S(2)}) collective-permute-start(f32[2,128]{1,0:T(2,128)S(1)} %get-tuple-element.24), channel_id=1, source_target_pairs={{28,0},{24,4},{20,8},{16,12},{12,16},{8,20},{4,24},{0,28},{29,1},{... | collective-permute-start | bytes 3080 | tf_op jit(solution)/shard_map/ppermute | solution.py:22
  10.0 7.9 %collective-permute-start.8 = (bf16[128,768]{1,0:T(8,128)(2,1)}, bf16[128,768]{1,0:T(8,128)(2,1)S(1)}, u32[]{:S(2)}, u32[]{:S(2)}) collective-permute-start(bf16[128,768]{1,0:T(8,128)(2,1)} %param.6), channel_id=1, source_target_pairs={{8,0},{12,4},{0,8},{4,12},{24,16},{28,20},{16,24},{20,28},{9,1},{1... | collective-permute-start | bytes 589832 | tf_op jit(solution)/shard_map/ppermute | solution.py:22
  11.6 12.3 %collective-permute-start.7 = (bf16[128,768]{1,0:T(8,128)(2,1)}, bf16[128,768]{1,0:T(8,128)(2,1)S(1)}, u32[]{:S(2)}, u32[]{:S(2)}) collective-permute-start(bf16[128,768]{1,0:T(8,128)(2,1)} %param.6), channel_id=1, source_target_pairs={{4,0},{0,4},{12,8},{8,12},{20,16},{16,20},{28,24},{24,28},{5,1},{1... | collective-permute-start | bytes 589832 | tf_op jit(solution)/shard_map/ppermute | solution.py:22
  11.7 11.7 %collective-permute-start.10 = (bf16[128,768]{1,0:T(8,128)(2,1)}, bf16[128,768]{1,0:T(8,128)(2,1)S(1)}, u32[]{:S(2)}, u32[]{:S(2)}) collective-permute-start(bf16[128,768]{1,0:T(8,128)(2,1)} %param.6), channel_id=1, source_target_pairs={{16,0},{20,4},{24,8},{28,12},{0,16},{4,20},{8,24},{12,28},{17,1},{... | collective-permute-start | bytes 589832 | tf_op jit(solution)/shard_map/ppermute | solution.py:22
  13.3 10.1 %collective-permute-start.12 = (bf16[128,768]{1,0:T(8,128)(2,1)}, bf16[128,768]{1,0:T(8,128)(2,1)S(1)}, u32[]{:S(2)}, u32[]{:S(2)}) collective-permute-start(bf16[128,768]{1,0:T(8,128)(2,1)} %param.6), channel_id=1, source_target_pairs={{24,0},{28,4},{16,8},{20,12},{8,16},{12,20},{0,24},{4,28},{25,1},{... | collective-permute-start | bytes 589832 | tf_op jit(solution)/shard_map/ppermute | solution.py:22
  18.0 6.0 %collective-permute-start.9 = (bf16[128,768]{1,0:T(8,128)(2,1)S(1)}, bf16[128,768]{1,0:T(8,128)(2,1)S(1)}, u32[]{:S(2)}, u32[]{:S(2)}) collective-permute-start(bf16[128,768]{1,0:T(8,128)(2,1)S(1)} %collective-permute-done.8), channel_id=1, source_target_pairs={{4,0},{0,4},{12,8},{8,12},{20,16},{16,20},{28,24},{24,28},{5,1},{1... | collective-permute-start | bytes 589832 | tf_op jit(solution)/shard_map/ppermute | solution.py:22
  23.4 1.4 %collective-permute-start.11 = (bf16[128,768]{1,0:T(8,128)(2,1)S(1)}, bf16[128,768]{1,0:T(8,128)(2,1)S(1)}, u32[]{:S(2)}, u32[]{:S(2)}) collective-permute-start(bf16[128,768]{1,0:T(8,128)(2,1)S(1)} %collective-permute-done.10), channel_id=1, source_target_pairs={{4,0},{0,4},{12,8},{8,12},{20,16},{16,20},{28,24},{24,28},{5,1},{1... | collective-permute-start | bytes 589832 | tf_op jit(solution)/shard_map/ppermute | solution.py:22
  23.4 1.7 %collective-permute-start.13 = (bf16[128,768]{1,0:T(8,128)(2,1)S(1)}, bf16[128,768]{1,0:T(8,128)(2,1)S(1)}, u32[]{:S(2)}, u32[]{:S(2)}) collective-permute-start(bf16[128,768]{1,0:T(8,128)(2,1)S(1)} %collective-permute-done.12), channel_id=1, source_target_pairs={{4,0},{0,4},{12,8},{8,12},{20,16},{16,20},{28,24},{24,28},{5,1},{1... | collective-permute-start | bytes 589832 | tf_op jit(solution)/shard_map/ppermute | solution.py:22
  26.2 0.7 %copy-start.2 = (f32[512]{0:T(512)S(1)}, f32[512]{0:T(512)}, u32[]{:S(2)}) copy-start(f32[512]{0:T(512)} %param.8) | copy-start | bytes 6148
  27.8 4.0 %collective-permute-start.20 = (f32[1024]{0:T(1024)S(1)}, f32[1024]{0:T(1024)S(1)}, u32[]{:S(2)}, u32[]{:S(2)}) collective-permute-start(f32[1024]{0:T(1024)S(1)} %log_add_fusion.1), channel_id=1, source_target_pairs={{28,0},{24,4},{20,8},{16,12},{12,16},{8,20},{4,24},{0,28},{29,1},{... | collective-permute-start | bytes 12296 | tf_op jit(solution)/shard_map/ppermute | solution.py:22
  29.2 5.9 %collective-permute-start.14 = (f32[1024]{0:T(1024)S(1)}, f32[1024]{0:T(1024)S(1)}, u32[]{:S(2)}, u32[]{:S(2)}) collective-permute-start(f32[1024]{0:T(1024)S(1)} %log_add_fusion.1), channel_id=1, source_target_pairs={{4,0},{0,4},{12,8},{8,12},{20,16},{16,20},{28,24},{24,28},{5,1},{1... | collective-permute-start | bytes 12296 | tf_op jit(solution)/shard_map/ppermute | solution.py:22
  29.5 5.5 %collective-permute-start.16 = (f32[1024]{0:T(1024)S(1)}, f32[1024]{0:T(1024)S(1)}, u32[]{:S(2)}, u32[]{:S(2)}) collective-permute-start(f32[1024]{0:T(1024)S(1)} %log_add_fusion.1), channel_id=1, source_target_pairs={{12,0},{8,4},{4,8},{0,12},{28,16},{24,20},{20,24},{16,28},{13,1},{... | collective-permute-start | bytes 12296 | tf_op jit(solution)/shard_map/ppermute | solution.py:22
  30.8 3.5 %collective-permute-start.18 = (f32[1024]{0:T(1024)S(1)}, f32[1024]{0:T(1024)S(1)}, u32[]{:S(2)}, u32[]{:S(2)}) collective-permute-start(f32[1024]{0:T(1024)S(1)} %log_add_fusion.1), channel_id=1, source_target_pairs={{20,0},{16,4},{28,8},{24,12},{4,16},{0,20},{12,24},{8,28},{21,1},{... | collective-permute-start | bytes 12296 | tf_op jit(solution)/shard_map/ppermute | solution.py:22
  31.2 6.8 %collective-permute-start.15 = (f32[1024]{0:T(1024)S(1)}, f32[1024]{0:T(1024)S(1)}, u32[]{:S(2)}, u32[]{:S(2)}) collective-permute-start(f32[1024]{0:T(1024)S(1)} %log_add_fusion.1), channel_id=1, source_target_pairs={{8,0},{12,4},{0,8},{4,12},{24,16},{28,20},{16,24},{20,28},{9,1},{1... | collective-permute-start | bytes 12296 | tf_op jit(solution)/shard_map/ppermute | solution.py:22
  31.8 6.2 %collective-permute-start.19 = (f32[1024]{0:T(1024)S(1)}, f32[1024]{0:T(1024)S(1)}, u32[]{:S(2)}, u32[]{:S(2)}) collective-permute-start(f32[1024]{0:T(1024)S(1)} %log_add_fusion.1), channel_id=1, source_target_pairs={{24,0},{28,4},{16,8},{20,12},{8,16},{12,20},{0,24},{4,28},{25,1},{... | collective-permute-start | bytes 12296 | tf_op jit(solution)/shard_map/ppermute | solution.py:22
  34.3 3.7 %collective-permute-start.17 = (f32[1024]{0:T(1024)S(1)}, f32[1024]{0:T(1024)S(1)}, u32[]{:S(2)}, u32[]{:S(2)}) collective-permute-start(f32[1024]{0:T(1024)S(1)} %log_add_fusion.1), channel_id=1, source_target_pairs={{16,0},{20,4},{24,8},{28,12},{0,16},{4,20},{8,24},{12,28},{17,1},{... | collective-permute-start | bytes 12296 | tf_op jit(solution)/shard_map/ppermute | solution.py:22
  38.2 4.9 %collective-permute-start.21 = (f32[1024]{0:T(1024)S(1)}, f32[1024]{0:T(1024)S(1)}, u32[]{:S(2)}, u32[]{:S(2)}) collective-permute-start(f32[1024]{0:T(1024)S(1)} %get-tuple-element.11), channel_id=1, source_target_pairs={{1,0},{0,1},{3,2},{2,3},{5,4},{4,5},{7,6},{6,7},{9,8},{8,9},{11,10... | collective-permute-start | bytes 12296 | tf_op jit(solution)/shard_map/ppermute | solution.py:22
  39.8 4.5 %collective-permute-start.22 = (f32[1024]{0:T(1024)S(1)}, f32[1024]{0:T(1024)S(1)}, u32[]{:S(2)}, u32[]{:S(2)}) collective-permute-start(f32[1024]{0:T(1024)S(1)} %get-tuple-element.11), channel_id=1, source_target_pairs={{2,0},{3,1},{0,2},{1,3},{6,4},{7,5},{4,6},{5,7},{10,8},{11,9},{8,1... | collective-permute-start | bytes 12296 | tf_op jit(solution)/shard_map/ppermute | solution.py:22
  42.4 5.4 %collective-permute-start.23 = (f32[1024]{0:T(1024)S(1)}, f32[1024]{0:T(1024)S(1)}, u32[]{:S(2)}, u32[]{:S(2)}) collective-permute-start(f32[1024]{0:T(1024)S(1)} %get-tuple-element.11), channel_id=1, source_target_pairs={{3,0},{2,1},{1,2},{0,3},{7,4},{6,5},{5,6},{4,7},{11,8},{10,9},{9,1... | collective-permute-start | bytes 12296 | tf_op jit(solution)/shard_map/ppermute | solution.py:22
  48.7 0.9 %copy-start.1 = (f32[512]{0:T(512)}, f32[512]{0:T(512)S(1)}, u32[]{:S(2)}) copy-start(f32[512]{0:T(512)S(1)} %multiply_subtract_fusion) | copy-start | bytes 6148
  48.7 15.4 %copy-start.3 = (f32[128]{0:T(128)S(1)}, f32[128]{0:T(128)}, u32[]{:S(2)}) copy-start(f32[128]{0:T(128)} %param.9) | copy-start | bytes 1540
  49.6 3.6 %collective-permute-start.24 = (f32[128]{0:T(128)S(1)}, f32[128]{0:T(128)S(1)}, u32[]{:S(2)}, u32[]{:S(2)}) collective-permute-start(f32[128]{0:T(128)S(1)} %get-tuple-element.9), channel_id=1, source_target_pairs={{4,0},{0,4},{12,8},{8,12},{20,16},{16,20},{28,24},{24,28},{5,1},{1... | collective-permute-start | bytes 1544 | tf_op jit(solution)/shard_map/ppermute | solution.py:22
  49.7 4.2 %collective-permute-start.25 = (f32[128]{0:T(128)S(1)}, f32[128]{0:T(128)S(1)}, u32[]{:S(2)}, u32[]{:S(2)}) collective-permute-start(f32[128]{0:T(128)S(1)} %get-tuple-element.8), channel_id=1, source_target_pairs={{8,0},{12,4},{0,8},{4,12},{24,16},{28,20},{16,24},{20,28},{9,1},{1... | collective-permute-start | bytes 1544 | tf_op jit(solution)/shard_map/ppermute | solution.py:22
  50.4 5.6 %collective-permute-start.26 = (f32[128]{0:T(128)S(1)}, f32[128]{0:T(128)S(1)}, u32[]{:S(2)}, u32[]{:S(2)}) collective-permute-start(f32[128]{0:T(128)S(1)} %get-tuple-element.7), channel_id=1, source_target_pairs={{12,0},{8,4},{4,8},{0,12},{28,16},{24,20},{20,24},{16,28},{13,1},{... | collective-permute-start | bytes 1544 | tf_op jit(solution)/shard_map/ppermute | solution.py:22
  51.6 4.4 %collective-permute-start.27 = (f32[128]{0:T(128)S(1)}, f32[128]{0:T(128)S(1)}, u32[]{:S(2)}, u32[]{:S(2)}) collective-permute-start(f32[128]{0:T(128)S(1)} %get-tuple-element.6), channel_id=1, source_target_pairs={{16,0},{20,4},{24,8},{28,12},{0,16},{4,20},{8,24},{12,28},{17,1},{... | collective-permute-start | bytes 1544 | tf_op jit(solution)/shard_map/ppermute | solution.py:22
  52.1 3.9 %collective-permute-start.28 = (f32[128]{0:T(128)S(1)}, f32[128]{0:T(128)S(1)}, u32[]{:S(2)}, u32[]{:S(2)}) collective-permute-start(f32[128]{0:T(128)S(1)} %get-tuple-element.5), channel_id=1, source_target_pairs={{20,0},{16,4},{28,8},{24,12},{4,16},{0,20},{12,24},{8,28},{21,1},{... | collective-permute-start | bytes 1544 | tf_op jit(solution)/shard_map/ppermute | solution.py:22
  53.3 4.4 %collective-permute-start.29 = (f32[128]{0:T(128)S(1)}, f32[128]{0:T(128)S(1)}, u32[]{:S(2)}, u32[]{:S(2)}) collective-permute-start(f32[128]{0:T(128)S(1)} %get-tuple-element.4), channel_id=1, source_target_pairs={{24,0},{28,4},{16,8},{20,12},{8,16},{12,20},{0,24},{4,28},{25,1},{... | collective-permute-start | bytes 1544 | tf_op jit(solution)/shard_map/ppermute | solution.py:22
  53.9 3.9 %collective-permute-start.30 = (f32[128]{0:T(128)S(1)}, f32[128]{0:T(128)S(1)}, u32[]{:S(2)}, u32[]{:S(2)}) collective-permute-start(f32[128]{0:T(128)S(1)} %get-tuple-element.3), channel_id=1, source_target_pairs={{28,0},{24,4},{20,8},{16,12},{12,16},{8,20},{4,24},{0,28},{29,1},{... | collective-permute-start | bytes 1544 | tf_op jit(solution)/shard_map/ppermute | solution.py:22
  57.9 4.5 %collective-permute-start.31 = (f32[128]{0:T(128)S(1)}, f32[128]{0:T(128)S(1)}, u32[]{:S(2)}, u32[]{:S(2)}) collective-permute-start(f32[128]{0:T(128)S(1)} %log_add_fusion.2), channel_id=1, source_target_pairs={{1,0},{0,1},{3,2},{2,3},{5,4},{4,5},{7,6},{6,7},{9,8},{8,9},{11,10... | collective-permute-start | bytes 1544 | tf_op jit(solution)/shard_map/ppermute | solution.py:22
  57.9 4.5 %collective-permute-start.32 = (f32[128]{0:T(128)S(1)}, f32[128]{0:T(128)S(1)}, u32[]{:S(2)}, u32[]{:S(2)}) collective-permute-start(f32[128]{0:T(128)S(1)} %log_add_fusion.2), channel_id=1, source_target_pairs={{2,0},{3,1},{0,2},{1,3},{6,4},{7,5},{4,6},{5,7},{10,8},{11,9},{8,1... | collective-permute-start | bytes 1544 | tf_op jit(solution)/shard_map/ppermute | solution.py:22
  58.7 5.3 %collective-permute-start.33 = (f32[128]{0:T(128)S(1)}, f32[128]{0:T(128)S(1)}, u32[]{:S(2)}, u32[]{:S(2)}) collective-permute-start(f32[128]{0:T(128)S(1)} %log_add_fusion.2), channel_id=1, source_target_pairs={{3,0},{2,1},{1,2},{0,3},{7,4},{6,5},{5,6},{4,7},{11,8},{10,9},{9,1... | collective-permute-start | bytes 1544 | tf_op jit(solution)/shard_map/ppermute | solution.py:22
